TPU v7x, 32 devices: a whole 2x2x4 slice. The times are simulated.
32 devices in a mesh: ka: 8 (over y, x, core), ga: 4 (over z).
Axes of the slice: x: 2, y: 2, z: 4, core: 2. Of those that a mesh axis runs over, the one named last changes fastest.
Arguments:
- band_coefs: bfloat16 [8, 16, 2, 2048], P('ka'), may hold values from -12 to 12
- screening: bfloat16 [1, 2048, 2048], P(None, 'ga'), may hold values from -0.125 to 0.125
- grid_index: int32 [2048], replicated, may hold values from 1 to 4095, as said below
Outputs:
- kernel: float32 [8, 1, 64, 128], P('ka', None, 'ga')
Inputs may be any that keep to these rules, and one draw needn't show every extreme that they name: `grid_index`: the 2048 values are distinct flat grid indices x * 16 * 16 + y * 16 + z; the anchor 0 never appears.
All inputs are finite; a program needn't handle non-finite values.
Results may differ from a plain program's by a relative error of at most 0.0049.
Values may be sent and summed in bfloat16 or wider, within the bound.
A program may use at most 64 MiB of HBM per device.

v0:
```python
import math

import jax
import jax.numpy as jnp
from jax import lax
from jax.sharding import PartitionSpec as P

NBND = 8
NG = 2048
NFFT = 16


def passed_along(value, axis, by):
    size = lax.axis_size(axis)
    return lax.ppermute(value, axis, [(i, (i + by) % size) for i in range(size)])


def make_table(phase, count, norm, sign):
    angle = phase.astype(jnp.float32) * (2.0 * math.pi / count)
    cosine = jnp.cos(angle) / norm
    sine = sign * jnp.sin(angle) / norm
    return jnp.stack([jnp.stack([cosine, sine]), jnp.stack([-sine, cosine])])


def line_table(count, sign):
    index = jnp.arange(count, dtype=jnp.int32)
    phase = index[:, None] * index[None, :] % count
    return make_table(phase, count, math.sqrt(count), sign)


def plane_table(count, sign):
    index = jnp.arange(count * count, dtype=jnp.int32)
    row_part = index // count
    col_part = index % count
    phase = (
        row_part[:, None] * row_part[None, :] % count
        + col_part[:, None] * col_part[None, :] % count
    ) % count
    return make_table(phase, count, float(count), sign)


def transform(field, tables):
    level = lax.Precision.HIGH
    field = jnp.einsum("bcxm,cdxu->bdum", field, tables[0], precision=level)
    return jnp.einsum("bcxm,cdmn->bdxn", field, tables[1], precision=level)


def to_grid(coeffs, grid_index):
    bands = coeffs.shape[0]
    waves = coeffs.shape[2]
    rows_flat = coeffs.reshape(bands * 2, waves)
    total = NFFT * NFFT * NFFT
    block = math.gcd(total, 512)
    count = total // block

    def one_block(first_point):
        points = first_point + jnp.arange(block, dtype=jnp.int32)
        selector = (grid_index[:, None] == points[None, :]).astype(jnp.bfloat16)
        return jnp.dot(rows_flat, selector, preferred_element_type=jnp.float32)

    starts = jnp.arange(count, dtype=jnp.int32) * block
    pieces = lax.map(one_block, starts)
    flat = jnp.transpose(pieces, (1, 0, 2)).reshape(bands, 2, total)
    return flat.reshape(bands, 2, NFFT, NFFT * NFFT)


def pair_density(first, second, grid_index, tables):
    real_part = first[:, None, 0] * second[None, :, 0] + first[:, None, 1] * second[None, :, 1]
    imag_part = first[:, None, 0] * second[None, :, 1] - first[:, None, 1] * second[None, :, 0]
    pairs = first.shape[0] * second.shape[0]
    field = jnp.stack([real_part, imag_part], axis=2).reshape(pairs, 2, NFFT, NFFT * NFFT)
    spectrum = transform(field, tables).reshape(pairs, 2, NFFT * NFFT * NFFT)
    return jnp.take(spectrum, grid_index, axis=2).astype(jnp.bfloat16)


def body(band_coefs, screening, grid_index):
    width = lax.axis_size("ga")
    place = lax.axis_index("ga")
    pair_count = NBND * NBND
    per_device = 2 * NBND // width
    start_own = place * per_device
    start_kind = start_own // NBND * NBND
    local = band_coefs[0]
    forward = (line_table(NFFT, -1.0), plane_table(NFFT, -1.0))
    inverse = (line_table(NFFT, 1.0), plane_table(NFFT, 1.0))
    own_bands = lax.dynamic_slice_in_dim(local, start_own, per_device, 0)
    first = transform(to_grid(own_bands, grid_index), inverse)
    moving = lax.dynamic_slice_in_dim(local, start_kind, NBND, 0)
    strip = screening.shape[1]
    scale = 1.0 / math.sqrt(NG)
    moving = passed_along(moving, "ka", 1)
    second = transform(to_grid(moving, grid_index), inverse)
    density = pair_density(first, second, grid_index, forward)
    weights = screening[0]
    strips = lax.all_to_all(density, "ga", split_axis=2, concat_axis=0, tiled=True)
    conduction = strips[pair_count:]
    piece = lax.all_gather(strips[:pair_count], "ga", axis=2, tiled=True)
    rows_flat = piece.reshape(piece.shape[0] * 2, piece.shape[2])
    mixed = lax.dot_general(
        rows_flat, weights, (((1,), (1,)), ((), ())), preferred_element_type=jnp.float32
    )
    screened = mixed.astype(jnp.bfloat16).reshape(pair_count, 2, strip)
    left = conduction.reshape(pair_count, 2 * strip)
    right_real = screened.reshape(pair_count, 2 * strip)
    right_imag = jnp.concatenate([screened[:, 1], -screened[:, 0]], axis=1)
    dims = (((1,), (1,)), ((), ()))
    real_block = lax.dot_general(left, right_real, dims, preferred_element_type=jnp.float32)
    imag_block = lax.dot_general(left, right_imag, dims, preferred_element_type=jnp.float32)
    terms = jnp.concatenate([real_block, imag_block], axis=1) * scale
    results = [lax.psum_scatter(terms, "ga", scatter_dimension=0, tiled=True)]
    return jnp.stack(results)[None]


def solution(mesh):
    return jax.shard_map(
        body,
        mesh=mesh,
        in_specs=(P("ka", None, None, None), P(None, "ga", None), P()),
        out_specs=P("ka", None, "ga", None),
        check_vma=False,
    )
```

profile of v0, /device:TPU:0, one launch (start us, length us, event | category | flops | bytes accessed | tf_op | source)
XLA Modules:
  0.0 167.2 jit_solution(15057987175276515074)
XLA Ops:
  6.5 1.7 dynamic-slice_bitcast_fusion
  8.9 0.8 constant_dynamic-slice_fusion
  9.7 1.3 fusion.62
  11.0 21.8 %while.20 = (s32[]{:T(128)}, f32[8,8,512]{2,1,0:T(8,128)S(1)}, s32[2048]{0:T(1024)}, s32[8]{0:T(128)S(1)}, bf16[8,2048]{1,0:T(8,128)(2,1)S(1)}, /*index=5*/s32[]{:T(128)}) while((s32[]{:T(128)}, f32[8,8,512]{2,1,0:T(8,128)S(1)}, s32[2048]{0:T(1024)}, s32[8]{0:T(128)S(1)}, bf16[8,2048]{1,0:T(8,128)(2,1)S(1)}, /*index=5*/s32[]{:T(128)}) %tuple.52), condition=%wide.region_1.2_spmd, body=%wide.region_0.1_spmd.sunk | while | flops 17826304 | bytes 61529 | solution.py:62
  11.6 0.6 iota_add_fusion.4
  12.2 1.5 fusion.94
  14.3 0.6 iota_add_fusion.4
  14.9 1.5 fusion.94
  17.0 0.6 iota_add_fusion.4
  17.7 1.5 fusion.94
  19.8 0.6 iota_add_fusion.4
  20.4 1.5 fusion.94
  22.5 0.6 iota_add_fusion.4
  23.1 1.5 fusion.94
  25.2 0.6 iota_add_fusion.4
  25.8 1.5 fusion.94
  27.9 0.6 iota_add_fusion.4
  28.6 1.5 fusion.94
  30.7 0.6 iota_add_fusion.4
  31.3 1.5 fusion.94
  33.4 1.3 broadcast_multiply_fusion.1
  36.0 1.2 fusion.34
  38.2 1.5 reshape.825
  39.7 28.6 %while.21 = (s32[]{:T(128)}, f32[8,16,512]{2,1,0:T(8,128)S(1)}, s32[2048]{0:T(1024)}, s32[8]{0:T(128)}, bf16[16,2048]{1,0:T(8,128)(2,1)}, /*index=5*/s32[]{:T(128)}) while((s32[]{:T(128)}, f32[8,16,512]{2,1,0:T(8,128)S(1)}, s32[2048]{0:T(1024)}, s32[8]{0:T(128)}, bf16[16,2048]{1,0:T(8,128)(2,1)}, /*index=5*/s32[]{:T(128)}) %tuple.58), condition=%wide.region_3.4_spmd, body=%wide.region_2.3_spmd.sunk | while | flops 34603520 | bytes 110681 | solution.py:62
  39.7 1.3 dynamic_slice.23
  41.0 0.6 iota_add_fusion.5
  41.6 1.7 fusion.97
  43.3 1.3 dynamic_slice.23
  44.6 0.6 iota_add_fusion.5
  45.2 1.7 fusion.97
  46.9 1.3 dynamic_slice.23
  48.1 0.6 iota_add_fusion.5
  48.8 1.7 fusion.97
  50.4 1.3 dynamic_slice.23
  51.7 0.6 iota_add_fusion.5
  52.4 1.7 fusion.97
  54.0 1.3 dynamic_slice.23
  55.3 0.6 iota_add_fusion.5
  55.9 1.7 fusion.97
  57.6 1.3 dynamic_slice.23
  58.9 0.6 iota_add_fusion.5
  59.5 1.7 fusion.97
  61.2 1.3 dynamic_slice.23
  62.4 0.6 iota_add_fusion.5
  63.1 1.7 fusion.97
  64.7 1.3 dynamic_slice.23
  66.0 0.6 iota_add_fusion.5
  66.7 1.7 fusion.97
  68.3 0.9 copy.20
  69.2 1.0 reshape.845
  70.2 1.0 convolution_bitcast_fusion.3
  71.9 0.6 convolution_bitcast_fusion.1
  72.9 1.4 convolution_bitcast_fusion
  74.4 3.7 %copy.46 = bf16[32,2,16,256]{0,1,3,2:T(2,128)(2,1)} copy(bf16[32,2,16,256]{3,0,2,1:T(8,128)(2,1)S(1)} %convolution_bitcast_fusion) | data formatting | bytes 1048576 | tf_op jit(solution)/shard_map/reshape | solution.py:72
  78.1 15.4 %gather_fusion = bf16[2048,32,2]{1,2,0:T(2,128)(2,1)} fusion(bf16[32,2,4096]{0,1,2:T(2,128)(2,1)} %bitcast.158, s32[2048]{0:T(1024)S(1)} %copy-done.6), kind=kCustom, calls=%fused_computation | custom fusion | bytes 532480 | tf_op jit(solution)/shard_map/jit(_take)/gather | solution.py:73
  93.5 9.8 %fusion.76 = bf16[2048,2,32]{2,1,0:T(2,128)(2,1)S(1)} fusion(bf16[2048,32,2]{1,2,0:T(2,128)(2,1)} %gather_fusion, pred[2048]{0:T(1024)(128)(4,1)S(1)} %copy-done.8), kind=kLoop, calls=%fused_computation.130 | loop fusion | flops 131072 | bytes 526336
  103.3 1.0 reshape.857
  104.2 15.8 %all_to_all.15 = bf16[4,2,16384]{2,1,0:T(2,128)(2,1)} all-to-all(bf16[4,2,16384]{2,1,0:T(2,128)(2,1)S(1)} %reshape.857), channel_id=1, replica_groups=mesh['ka'=8,'ga'=4] {'ga'}, dimensions={0} | all-to-all | bytes 524288 | tf_op jit(solution)/shard_map/all_to_all | solution.py:95
  120.0 3.0 %reshape.858 = bf16[2048,2,32]{2,1,0:T(2,128)(2,1)S(1)} reshape(bf16[4,2,16384]{2,1,0:T(2,128)(2,1)} %all_to_all.15) | data formatting | bytes 524288
  123.1 0.7 copy.26
  123.8 16.0 %all_gather.3 = bf16[64,2,2048]{2,0,1:T(8,128)(2,1)S(1)} all-gather(bf16[64,2,512]{2,0,1:T(8,128)(2,1)S(1)} %bitcast.164), channel_id=1, replica_groups=mesh['ka'=8,'ga'=4] {'ga'}, dimensions={2}, use_global_device_ids=true | all-gather | bytes 655360 | tf_op jit(solution)/shard_map/all_gather | solution.py:97
  140.5 0.8 fusion.22
  142.2 0.7 maximum_multiply_fusion
  142.9 17.4 %reduce-scatter.2.cloned.1.call-done = f32[16,128]{1,0:T(8,128)} async-done(((f32[64,128]{1,0:T(8,128)}), f32[16,128]{1,0:T(8,128)}) %reduce-scatter.2.cloned.1.call-update) | async-done | bytes 8208 | tf_op jit(solution)/shard_map/reduce_scatter | solution.py:110
  (62 shorter events, 10.9 us)
Async XLA Ops:
  6.5 133.9 %copy-start = (bf16[1,512,2048]{2,1,0:T(8,128)(2,1)S(1)}, bf16[1,512,2048]{2,1,0:T(8,128)(2,1)}, u32[]{:S(2)}) copy-start(bf16[1,512,2048]{2,1,0:T(8,128)(2,1)} %param.8) | copy-start | bytes 6291460
  6.5 153.8 %reduce-scatter.2.cloned.1.call-start = ((), (), s32[]{:S(2)}) async-start(), calls=%async_computation.2 | async-start | bytes 40960 | tf_op jit(solution)/shard_map/reduce_scatter | solution.py:110
  8.2 30.0 %collective-permute-start = (bf16[8,2,2048]{2,1,0:T(2,128)(2,1)}, bf16[8,2,2048]{2,1,0:T(2,128)(2,1)}, u32[]{:S(2)}, u32[]{:S(2)}) collective-permute-start(bf16[8,2,2048]{2,1,0:T(2,128)(2,1)} %dynamic-slice_bitcast_fusion), channel_id=1, source_target_pairs={{0,4},{4,8},{8,12},{12,16},{16,20},{20,24},{24,28},{28,0},{1,5},{5... | collective-permute-start | bytes 196616 | tf_op jit(solution)/shard_map/ppermute | solution.py:15
  32.8 0.5 copy-start.9
  35.4 0.6 copy-start.3
  36.0 1.6 copy-start.7
  70.2 1.7 %copy-start.4 = (f32[1,2,16,16]{2,3,1,0:T(8,128)S(1)}, f32[1,2,16,16]{2,3,1,0:T(8,128)}, u32[]{:S(2)}) copy-start(f32[1,2,16,16]{2,3,1,0:T(8,128)} %get-tuple-element.95) | copy-start | bytes 6148
  70.2 1.7 %copy-start.5 = (f32[1,2,16,16]{2,3,1,0:T(8,128)S(1)}, f32[1,2,16,16]{2,3,1,0:T(8,128)}, u32[]{:S(2)}) copy-start(f32[1,2,16,16]{2,3,1,0:T(8,128)} %get-tuple-element.98) | copy-start | bytes 6148
  71.7 1.0 copy-start.1
  71.7 1.2 copy-start.2
  72.9 5.2 %copy-start.6 = (s32[2048]{0:T(1024)S(1)}, s32[2048]{0:T(1024)}, u32[]{:S(2)}) copy-start(s32[2048]{0:T(1024)} %fusion.62) | copy-start | bytes 24580
  74.3 19.2 %copy-start.8 = (pred[2048]{0:T(1024)(128)(4,1)S(1)}, pred[2048]{0:T(1024)(128)(4,1)}, u32[]{:S(2)}) copy-start(pred[2048]{0:T(1024)(128)(4,1)} %compare_and_fusion) | copy-start | bytes 6148
Sparse Core Ops, SparseCore 0:
  143.1 17.2 reduce-scatter.1
where the time goes:
time: 169 us; the launch traced here: 167 us
  local copies, waits for them, and re-layouts  47.2 us (28%)
  blocking collectives  31.7 us (19%)
  matrix products  30.6 us (18%)
  other arithmetic  25.9 us (15%)
  waiting for transfers between devices  17.4 us (10%)
  between operations  13.7 us (8%)
    dot_general x16, matrix products, one_block(): return jnp.dot(rows_flat, selector, preferred_element_type=jnp.float32)  25.2 us
    reduce_scatter x1, waiting for transfers between devices, body(): results = [lax.psum_scatter(terms, 'ga', scatter_dimension=0, tiled=True)]  17.4 us
    all_gather x1, blocking collectives, body(): piece = lax.all_gather(strips[:pair_count], 'ga', axis=2, tiled=True)  16 us
    all_to_all x1, blocking collectives, body(): lax.all_to_all(density, 'ga', split_axis=2, concat_axis=0, tiled=True)  15.8 us
    gather x1, local copies, waits for them, and re-layouts, pair_density(): return jnp.take(spectrum, grid_index, axis=2).astype(jnp.bfloat16)  15.4 us
    dynamic_slice x16, local copies, waits for them, and re-layouts, to_grid(): pieces = lax.map(one_block, starts)  15 us
    add x16, other arithmetic, one_block(): points = first_point + jnp.arange(block, dtype=jnp.int32)  10.1 us
    unnamed x1, other arithmetic  9.75 us
  transfers between devices with their start and end apart: 2, of which 1 were waited for; matrix products, arithmetic and copies ran while one was open for 17% of the time, Pallas kernels for 0%

commit v1 on v0

v1 whole, which is shorter than its diff:
```python
import functools
import math

import jax
import jax.numpy as jnp
import numpy as np
from jax import lax
from jax.experimental import pallas as pl
from jax.experimental.pallas import tpu as pltpu
from jax.sharding import PartitionSpec as P

NBND = 8
NFFT = 16
PLANE = NFFT * NFFT
GRID = NFFT * PLANE
PAIRS = NBND * NBND
LANES = 2 * PAIRS
BANDS = 4 * NBND
BF = jnp.bfloat16
F32 = jnp.float32
MESH = pl.DeviceIdType.MESH


def radix4(parts, sign):
    (ar, ai), (br, bi), (cr, ci), (dr, di) = parts
    sr, si = ar + cr, ai + ci
    tr, ti = ar - cr, ai - ci
    ur, ui = br + dr, bi + di
    vr, vi = br - dr, bi - di
    first = (sr + ur, si + ui)
    third = (sr - ur, si - ui)
    plus = (tr - vi, ti + vr)
    minus = (tr + vi, ti - vr)
    if sign > 0:
        return [first, plus, third, minus]
    return [first, minus, third, plus]


def twiddle(value, power, sign):
    re, im = value
    power = (power * (1 if sign > 0 else -1)) % 16
    if power == 0:
        return value
    if power == 4:
        return (-im, re)
    if power == 12:
        return (im, -re)
    cosine = math.cos(2.0 * math.pi * power / 16)
    sine = math.sin(2.0 * math.pi * power / 16)
    if power % 4 == 2:
        half = math.sqrt(0.5)
        p = 1.0 if cosine > 0 else -1.0
        q = 1.0 if sine > 0 else -1.0
        if p == q:
            return ((re - im) * (p * half), (re + im) * (p * half))
        return ((re + im) * (p * half), (im - re) * (p * half))
    return (re * cosine - im * sine, re * sine + im * cosine)


def fft16(values, sign):
    inner = [radix4([values[4 * j + i] for j in range(4)], sign) for i in range(4)]
    out = [None] * 16
    for k1 in range(4):
        parts = [twiddle(inner[i][k1], i * k1, sign) for i in range(4)]
        for k2, got in enumerate(radix4(parts, sign)):
            out[k1 + 4 * k2] = got
    return out


def tables():
    group = np.arange(LANES) // BANDS
    band = np.arange(LANES) % BANDS
    same = (band[:, None] == band[None, :]).astype(np.float64)
    mats = []
    for k1 in range(4):
        angle = 2.0 * np.pi * (group[:, None] * (k1 + 4 * group[None, :]) % 16) / 16
        c, s = np.cos(angle) * same, np.sin(angle) * same
        mats.append(np.block([[c, s], [-s, c]]))
    full = np.stack(mats).astype(np.float32)
    high = full.astype(BF)
    low = (full - high.astype(np.float32)).astype(BF)
    lane = np.arange(LANES)
    kind, pair = lane // PAIRS, lane % PAIRS
    first = kind * NBND + pair // NBND
    second = 2 * NBND + kind * NBND + pair % NBND
    spread = []
    for g in range(4):
        here = (group == g)[:, None]
        block = np.concatenate(
            [here & (band[:, None] == first[None, :]), here & (band[:, None] == second[None, :])], axis=1
        )
        spread.append(np.concatenate([block, block], axis=0) * 0.125)
    return high, low, np.stack(spread).astype(BF)


def split(value):
    high = value.astype(BF)
    return high, (value - high.astype(F32)).astype(BF)


def compute(strip, rows, here_ref, there_ref, vec_ref, idx_ref, w_ref, mh_ref, ml_ref, e_ref, out_ref,
            pre, pim, qre, qim, vgrid, cgrid, vpick, cpick):
    waves = vec_ref.shape[1]
    index = vec_ref[...]
    cut_x = index // PLANE
    cut_n = index % PLANE
    points = lax.broadcasted_iota(jnp.int32, (PLANE, waves), 0)
    onehot = jnp.where(points == cut_n, 1.0 / 64, 0.0).astype(BF)
    coefs = [
        jnp.concatenate([here_ref[:, c, :], there_ref[:, c, :]], axis=0) for c in range(2)
    ]
    for j in range(4):
        masks = [(cut_x == 4 * j + i).astype(F32).astype(BF) for i in range(4)]
        block = jnp.concatenate([coefs[c] * masks[i] for c in range(2) for i in range(4)], axis=0)
        field = lax.dot_general(onehot, block, (((1,), (1,)), ((), ())), preferred_element_type=F32)
        pre[pl.ds(j * PLANE, PLANE), :] = field[:, :LANES]
        pim[pl.ds(j * PLANE, PLANE), :] = field[:, LANES:]

    @pl.loop(0, 8)
    def _(step):
        base = (step // 2) * PLANE + (step % 2) * 8
        at = [pl.ds(pl.multiple_of(base + y * NFFT, 8), 8) for y in range(NFFT)]
        for y, (re, im) in enumerate(fft16([(pre[a, :], pim[a, :]) for a in at], 1)):
            pre[at[y], :] = re
            pim[at[y], :] = im

    @pl.loop(0, 8)
    def _(step):
        base = pl.multiple_of(step * 128, 128)
        got = fft16(
            [(pre[pl.ds(base + z, 8, stride=NFFT), :], pim[pl.ds(base + z, 8, stride=NFFT), :]) for z in range(NFFT)], 1
        )
        for z, (re, im) in enumerate(got):
            pre[pl.ds(base + z * 8, 8), :] = re
            pim[pl.ds(base + z * 8, 8), :] = im

    quarters = [(pre[pl.ds(j * PLANE, PLANE), :], pim[pl.ds(j * PLANE, PLANE), :]) for j in range(4)]
    for k1, (re, im) in enumerate(radix4(quarters, 1)):
        high, low = split(jnp.concatenate([re, im], axis=1))
        mixed = (
            jnp.dot(high, mh_ref[k1], preferred_element_type=F32)
            + jnp.dot(low, mh_ref[k1], preferred_element_type=F32)
            + jnp.dot(high, ml_ref[k1], preferred_element_type=F32)
        )
        left_re = jnp.concatenate(split(mixed[:, :LANES]), axis=1)
        left_im = jnp.concatenate(split(mixed[:, LANES:]), axis=1)
        for g in range(4):
            real = jnp.dot(left_re, e_ref[g], preferred_element_type=F32)
            imag = jnp.dot(left_im, e_ref[g], preferred_element_type=F32)
            ar, br = real[:, :LANES], real[:, LANES:]
            ai, bi = imag[:, :LANES], imag[:, LANES:]
            at = pl.ds((k1 + 4 * g) * PLANE, PLANE)
            qre[at, :] = ar * br + ai * bi
            qim[at, :] = ar * bi - ai * br

    @pl.loop(0, 32)
    def _(step):
        at = [pl.ds(pl.multiple_of(x * PLANE + step * 8, 8), 8) for x in range(NFFT)]
        for x, (re, im) in enumerate(fft16([(qre[a, :], qim[a, :]) for a in at], -1)):
            qre[at[x], :] = re
            qim[at[x], :] = im

    @pl.loop(0, 32)
    def _(step):
        at = [pl.ds(pl.multiple_of(step * 128 + z * 8, 8), 8) for z in range(NFFT)]
        for z, (re, im) in enumerate(fft16([(qre[a, :], qim[a, :]) for a in at], -1)):
            qre[at[z], :] = re
            qim[at[z], :] = im

    left_half = lax.broadcasted_iota(jnp.int32, (8, LANES), 1) < PAIRS

    @pl.loop(0, 32)
    def _(step):
        plane = (step // 2) * PLANE
        half = step % 2
        take = [
            pl.ds(plane + (y // 8) * 128 + half * 64 + y % 8, 8, stride=8) for y in range(NFFT)
        ]
        for y, (re, im) in enumerate(fft16([(qre[a, :], qim[a, :]) for a in take], -1)):
            at = pl.ds(pl.multiple_of(plane + y * NFFT + half * 8, 8), 8)
            vgrid[at, :] = jnp.where(left_half, re, pltpu.roll(im, PAIRS, 1))
            cgrid[at, :] = jnp.where(left_half, pltpu.roll(re, PAIRS, 1), im)

    @pl.loop(0, waves // 32)
    def _(step):
        for u in range(32):
            g = step * 32 + u
            vpick[pl.ds(g, 1), :] = vgrid[pl.ds(idx_ref[g], 1), :]

    start = lax.axis_index("ga") * strip

    @pl.loop(0, strip // 32)
    def _(step):
        for u in range(32):
            g = step * 32 + u
            cpick[pl.ds(g, 1), :] = cgrid[pl.ds(idx_ref[start + g], 1), :]

    screened = jnp.dot(w_ref[...], vpick[...].astype(BF), preferred_element_type=F32).astype(BF)
    left = cpick[...].T.astype(BF)
    cross = jnp.dot(left, screened, preferred_element_type=F32)
    top, bottom = cross[:PAIRS], pltpu.roll(cross[PAIRS:], PAIRS, 1)
    lane = lax.broadcasted_iota(jnp.int32, (PAIRS, LANES), 1)
    total = jnp.where(lane < PAIRS, top + bottom, top - bottom) * (1.0 / math.sqrt(waves))
    for d in range(PAIRS // rows):
        out_ref[d] = total[d * rows:(d + 1) * rows]


def scatter_sum(width, x_ref, out_ref, slots, send_sem, recv_sem):
    me = lax.axis_index("ga")
    barrier = pltpu.get_barrier_semaphore()
    for step in range(1, width):
        pl.semaphore_signal(barrier, inc=1, device_id={"ga": lax.rem(me + step, width)}, device_id_type=MESH)
    pl.semaphore_wait(barrier, width - 1)
    copies = []
    for step in range(1, width):
        peer = lax.rem(me + step, width)
        copy = pltpu.make_async_remote_copy(
            src_ref=x_ref.at[peer],
            dst_ref=slots.at[step - 1],
            send_sem=send_sem.at[step - 1],
            recv_sem=recv_sem.at[step - 1],
            device_id={"ga": peer},
            device_id_type=MESH,
        )
        copy.start()
        copies.append(copy)
    total = x_ref[me]
    for step, copy in enumerate(copies):
        copy.wait_recv()
        total = total + slots[step]
    out_ref[...] = total
    for copy in copies:
        copy.wait_send()


def body(band_coefs, screening, grid_index):
    width = lax.axis_size("ga")
    count = lax.axis_size("ka")
    strip, waves = screening.shape[1:]
    rows = PAIRS // width
    here = band_coefs[0]
    there = lax.ppermute(here, "ka", [(i, (i + 1) % count) for i in range(count)])
    high, low, spread = tables()
    vmem = pl.BlockSpec(memory_space=pltpu.VMEM)
    smem = pl.BlockSpec(memory_space=pltpu.SMEM)
    terms = pl.pallas_call(
        functools.partial(compute, strip, rows),
        out_shape=jax.ShapeDtypeStruct((width, rows, LANES), F32),
        in_specs=[vmem, vmem, vmem, smem, vmem, vmem, vmem, vmem],
        out_specs=vmem,
        scratch_shapes=[
            pltpu.VMEM((4 * PLANE, LANES), F32),
            pltpu.VMEM((4 * PLANE, LANES), F32),
            pltpu.VMEM((GRID, LANES), F32),
            pltpu.VMEM((GRID, LANES), F32),
            pltpu.VMEM((GRID, LANES), F32),
            pltpu.VMEM((GRID, LANES), F32),
            pltpu.VMEM((waves, LANES), F32),
            pltpu.VMEM((strip, LANES), F32),
        ],
        compiler_params=pltpu.CompilerParams(vmem_limit_bytes=48 * 1024 * 1024),
    )(here, there, grid_index[None], grid_index, screening[0], jnp.asarray(high), jnp.asarray(low), jnp.asarray(spread))
    result = pl.pallas_call(
        functools.partial(scatter_sum, width),
        out_shape=jax.ShapeDtypeStruct((rows, LANES), F32),
        in_specs=[vmem],
        out_specs=vmem,
        scratch_shapes=[
            pltpu.VMEM((width - 1, rows, LANES), F32),
            pltpu.SemaphoreType.DMA((width - 1,)),
            pltpu.SemaphoreType.DMA((width - 1,)),
        ],
        compiler_params=pltpu.CompilerParams(collective_id=0, has_side_effects=True),
    )(terms)
    return result[None, None]


def solution(mesh):
    return jax.shard_map(
        body,
        mesh=mesh,
        in_specs=(P("ka", None, None, None), P(None, "ga", None), P()),
        out_specs=P("ka", None, "ga", None),
        check_vma=False,
    )
```

time: 169 us -> 38.7 us (0.23)
  local copies, waits for them, and re-layouts: 47.2 us -> 8.2 us
  blocking collectives: 31.7 us -> 0 us
  matrix products: 30.6 us -> 0 us
  other arithmetic: 25.9 us -> 0 us
  Pallas kernels: 0 us -> 23.8 us
  between operations: 13.7 us -> 0.03 us
  waiting for transfers between devices: 17.4 us -> 5.74 us
    dot_general x25 -> x0, matrix products: 30.6 us -> none  [the longest x16 25.2 us: one_block(): return jnp.dot(rows_flat, selector, preferred_element_type=jnp.float32)]
    pallas_call x0 -> x2, Pallas kernels: none -> 23.8 us  [the longest x1 15.7 us: body(): pl.pallas_call(functools.partial(compute, strip, rows), out_shape=jax.Sha...]
    dynamic_slice x18 -> x0, local copies, waits for them, and re-layouts: 17.4 us -> none  [the longest x16 15 us: to_grid(): pieces = lax.map(one_block, starts)]
    reduce_scatter x1 -> x0, waiting for transfers between devices: 17.4 us -> none  [body(): results = [lax.psum_scatter(terms, 'ga', scatter_dimension=0, tiled=True)]]
    all_gather x1 -> x0, blocking collectives: 16 us -> none  [body(): piece = lax.all_gather(strips[:pair_count], 'ga', axis=2, tiled=True)]
    all_to_all x1 -> x0, blocking collectives: 15.8 us -> none  [body(): lax.all_to_all(density, 'ga', split_axis=2, concat_axis=0, tiled=True)]
    gather x1 -> x0, local copies, waits for them, and re-layouts: 15.4 us -> none  [pair_density(): return jnp.take(spectrum, grid_index, axis=2).astype(jnp.bfloat16)]
    add x17 -> x0, other arithmetic: 10.2 us -> none  [the longest x16 10.1 us: one_block(): points = first_point + jnp.arange(block, dtype=jnp.int32)]
  transfers between devices with their start and end apart: 2 -> 1, of which waited for: 1 -> 1; matrix products, arithmetic and copies ran while one was open for 17% -> 0% of each run, Pallas kernels for 0% -> 0%
where the time goes in v1:
time: 38.7 us; the launch traced here: 38.2 us
  Pallas kernels  23.8 us (61%)
  local copies, waits for them, and re-layouts  8.2 us (21%)
  waiting for transfers between devices  5.74 us (15%)
  starting transfers between devices  0.45 us (1%)
    pallas_call x1, Pallas kernels, body(): pl.pallas_call(functools.partial(compute, strip, rows), out_shape=jax.Sha...  15.7 us
    unnamed x15, local copies, waits for them, and re-layouts  8.2 us
    pallas_call x1, Pallas kernels, body(): pl.pallas_call(functools.partial(scatter_sum, width), out_shape=jax.Shape...  8.07 us
    ppermute x1, waiting for transfers between devices, body(): lax.ppermute(here, 'ka', [(i, (i + 1) % count) for i in range(count)])  5.74 us
  transfers between devices with their start and end apart: 1, of which 1 were waited for; matrix products, arithmetic and copies ran while one was open for 0% of the time, Pallas kernels for 0%

profile of v1, /device:TPU:0, one launch (start us, length us, event | category | flops | bytes accessed | tf_op | source)
XLA Modules:
  0.0 38.2 jit_solution(13553603614385523813)
XLA Ops:
  0.0 0.5 %collective-permute-start = (bf16[16,2,2048]{2,1,0:T(2,128)(2,1)}, bf16[16,2,2048]{2,1,0:T(2,128)(2,1)S(1)}, u32[]{:S(2)}, u32[]{:S(2)}) collective-permute-start(bf16[16,2,2048]{2,1,0:T(2,128)(2,1)} %bitcast.5), channel_id=1, source_target_pairs={{0,4},{4,8},{8,12},{12,16},{16,20},{20,24},{24,28},{28,0},{1,5},{5... | collective-permute-start | bytes 393224 | tf_op jit(solution)/shard_map/ppermute | solution.py:242
  0.5 5.7 %collective-permute-done.there_ref = bf16[16,2,2048]{2,1,0:T(2,128)(2,1)S(1)} collective-permute-done((bf16[16,2,2048]{2,1,0:T(2,128)(2,1)}, bf16[16,2,2048]{2,1,0:T(2,128)(2,1)S(1)}, u32[]{:S(2)}, u32[]{:S(2)}) %collective-permute-start) | collective-permute-done | bytes 131104 | tf_op jit(solution)/shard_map/ppermute | solution.py:242
  6.2 0.0 copy-start
  6.2 1.6 %copy-done = bf16[1,512,2048]{2,1,0:T(8,128)(2,1)S(1)} copy-done((bf16[1,512,2048]{2,1,0:T(8,128)(2,1)S(1)}, bf16[1,512,2048]{2,1,0:T(8,128)(2,1)}, u32[]{:S(2)}) %copy-start) | copy-done | bytes 2097176
  7.8 0.0 copy-start.1
  7.8 1.0 %copy-done.1 = bf16[4,256,256]{2,1,0:T(8,128)(2,1)S(1)} copy-done((bf16[4,256,256]{2,1,0:T(8,128)(2,1)S(1)}, bf16[4,256,256]{2,1,0:T(8,128)(2,1)}, u32[]{:S(2)}) %copy-start.1) | copy-done | bytes 524312
  8.8 0.0 copy-start.2
  8.8 1.0 %copy-done.2 = bf16[4,256,256]{2,1,0:T(8,128)(2,1)S(1)} copy-done((bf16[4,256,256]{2,1,0:T(8,128)(2,1)S(1)}, bf16[4,256,256]{2,1,0:T(8,128)(2,1)}, u32[]{:S(2)}) %copy-start.2) | copy-done | bytes 524312
  9.9 0.0 copy-start.3
  9.9 1.0 %copy-done.3 = bf16[4,256,256]{2,1,0:T(8,128)(2,1)S(1)} copy-done((bf16[4,256,256]{2,1,0:T(8,128)(2,1)S(1)}, bf16[4,256,256]{2,1,0:T(8,128)(2,1)}, u32[]{:S(2)}) %copy-start.3) | copy-done | bytes 524312
  10.9 0.0 copy-start.5
  10.9 0.9 %copy-done.5 = bf16[1,16,2,2048]{3,2,1,0:T(2,128)(2,1)S(1)} copy-done((bf16[1,16,2,2048]{3,2,1,0:T(2,128)(2,1)S(1)}, bf16[1,16,2,2048]{3,2,1,0:T(2,128)(2,1)}, u32[]{:S(2)}) %copy-start.5) | copy-done | bytes 131096
  11.8 0.0 copy-start.6
  11.8 0.7 %copy-done.6 = s32[2048]{0:T(1024)S(1)} copy-done((s32[2048]{0:T(1024)S(1)}, s32[2048]{0:T(1024)}, u32[]{:S(2)}) %copy-start.6) | copy-done | bytes 8216
  12.5 15.7 %shard_map.64.x_ref = f32[4,16,128]{2,1,0:T(8,128)S(1)} custom-call(bf16[16,2,2048]{2,1,0:T(2,128)(2,1)S(1)} %bitcast.6, bf16[16,2,2048]{2,1,0:T(2,128)(2,1)S(1)} %collective-permute-done.there_ref, s32[1,2048]{1,0:T(1,128)S(1)} %bitcast.7, s32[2048]{0:T(1024)S(1)} %copy-done.6, bf16[512,2048]{1,0:T(8,128)(2,1)S(1)} %bitcast.4, ...), custom_call_target="tpu_custom_call" | custom-call | tf_op jit(solution)/shard_map/pallas_call | solution.py:246
  28.2 0.0 copy-start.4
  28.3 0.6 %copy-done.4 = f32[4,16,128]{2,1,0:T(8,128)} copy-done((f32[4,16,128]{2,1,0:T(8,128)}, f32[4,16,128]{2,1,0:T(8,128)S(1)}, u32[]{:S(2)}) %copy-start.4) | copy-done | bytes 32792
  28.8 8.1 %shard_map.65 = f32[16,128]{1,0:T(8,128)} custom-call(f32[4,16,128]{2,1,0:T(8,128)} %copy-done.4), custom_call_target="tpu_custom_call" | custom-call | tf_op jit(solution)/shard_map/pallas_call | solution.py:263
  36.9 1.3 %copy.8 = f32[1,1,16,128]{3,2,1,0:T(8,128)} copy(f32[1,1,16,128]{3,2,1,0:T(8,128)} %bitcast.8) | data formatting | bytes 16384
Async XLA Ops:
  0.0 6.2 %collective-permute-start = (bf16[16,2,2048]{2,1,0:T(2,128)(2,1)}, bf16[16,2,2048]{2,1,0:T(2,128)(2,1)S(1)}, u32[]{:S(2)}, u32[]{:S(2)}) collective-permute-start(bf16[16,2,2048]{2,1,0:T(2,128)(2,1)} %bitcast.5), channel_id=1, source_target_pairs={{0,4},{4,8},{8,12},{12,16},{16,20},{20,24},{24,28},{28,0},{1,5},{5... | collective-permute-start | bytes 393224 | tf_op jit(solution)/shard_map/ppermute | solution.py:242
  6.2 1.6 %copy-start = (bf16[1,512,2048]{2,1,0:T(8,128)(2,1)S(1)}, bf16[1,512,2048]{2,1,0:T(8,128)(2,1)}, u32[]{:S(2)}) copy-start(bf16[1,512,2048]{2,1,0:T(8,128)(2,1)} %param.7) | copy-start | bytes 6291460
  7.8 1.0 %copy-start.1 = (bf16[4,256,256]{2,1,0:T(8,128)(2,1)S(1)}, bf16[4,256,256]{2,1,0:T(8,128)(2,1)}, u32[]{:S(2)}) copy-start(bf16[4,256,256]{2,1,0:T(8,128)(2,1)} %constant.8.clone.e_ref) | copy-start | bytes 1572868
  8.8 1.0 %copy-start.2 = (bf16[4,256,256]{2,1,0:T(8,128)(2,1)S(1)}, bf16[4,256,256]{2,1,0:T(8,128)(2,1)}, u32[]{:S(2)}) copy-start(bf16[4,256,256]{2,1,0:T(8,128)(2,1)} %constant.7.clone.ml_ref) | copy-start | bytes 1572868
  9.9 1.0 %copy-start.3 = (bf16[4,256,256]{2,1,0:T(8,128)(2,1)S(1)}, bf16[4,256,256]{2,1,0:T(8,128)(2,1)}, u32[]{:S(2)}) copy-start(bf16[4,256,256]{2,1,0:T(8,128)(2,1)} %constant.6.clone.mh_ref) | copy-start | bytes 1572868
  10.9 0.9 %copy-start.5 = (bf16[1,16,2,2048]{3,2,1,0:T(2,128)(2,1)S(1)}, bf16[1,16,2,2048]{3,2,1,0:T(2,128)(2,1)}, u32[]{:S(2)}) copy-start(bf16[1,16,2,2048]{3,2,1,0:T(2,128)(2,1)} %param.6) | copy-start | bytes 393220
  11.8 0.7 %copy-start.6 = (s32[2048]{0:T(1024)S(1)}, s32[2048]{0:T(1024)}, u32[]{:S(2)}) copy-start(s32[2048]{0:T(1024)} %idx_ref.1) | copy-start | bytes 24580
  28.2 0.6 %copy-start.4 = (f32[4,16,128]{2,1,0:T(8,128)}, f32[4,16,128]{2,1,0:T(8,128)S(1)}, u32[]{:S(2)}) copy-start(f32[4,16,128]{2,1,0:T(8,128)S(1)} %shard_map.64.x_ref) | copy-start | bytes 98308

commit v2 on v1

--- a/solution.py
+++ b/solution.py
@@ -68,8 +68,9 @@
 
 
 def tables():
-    group = np.arange(LANES) // BANDS
-    band = np.arange(LANES) % BANDS
+    half = BANDS // 2
+    group = np.arange(LANES) // half % 4
+    band = np.arange(LANES) // PAIRS * half + np.arange(LANES) % half
     same = (band[:, None] == band[None, :]).astype(np.float64)
     mats = []
     for k1 in range(4):
@@ -98,23 +99,61 @@
     return high, (value - high.astype(F32)).astype(BF)
 
 
-def compute(strip, rows, here_ref, there_ref, vec_ref, idx_ref, w_ref, mh_ref, ml_ref, e_ref, out_ref,
-            pre, pim, qre, qim, vgrid, cgrid, vpick, cpick):
+def scattered(coef_ref, cut_x, onehot, first):
+    parts = [coef_ref[:, c, :] for c in range(2)]
+    block = []
+    for j in (first, first + 1):
+        masks = [(cut_x == 4 * j + i).astype(F32).astype(BF) for i in range(4)]
+        block += [parts[c] * masks[i] for c in range(2) for i in range(4)]
+    block = jnp.concatenate(block, axis=0)
+    return lax.dot_general(onehot, block, (((1,), (1,)), ((), ())), preferred_element_type=F32)
+
+
+def compute(width, count, strip, rows, coef_hbm, vec_hbm, idx_hbm, w_hbm, mh_hbm, ml_hbm, e_hbm, out_ref,
+            here_ref, there_ref, vec_ref, idx_ref, w_ref, mh_ref, ml_ref, e_ref,
+            own, pre, pim, qre, qim, vgrid, cgrid, vpick, cpick, blocks, slots,
+            in_sem, ring_send, ring_recv, send_sem, recv_sem):
+    me = lax.axis_index("ga")
+    point = lax.axis_index("ka")
+    pairs = [(vec_hbm, vec_ref), (coef_hbm, here_ref), (idx_hbm, idx_ref), (mh_hbm, mh_ref), (ml_hbm, ml_ref),
+             (e_hbm, e_ref), (w_hbm, w_ref)]
+    fetch = [pltpu.make_async_copy(src, dst, in_sem.at[n]) for n, (src, dst) in enumerate(pairs)]
+    for copy in fetch:
+        copy.start()
+    barrier = pltpu.get_barrier_semaphore()
+    left_point = lax.rem(point + count - 1, count)
+    pl.semaphore_signal(barrier, inc=1, device_id={"ka": left_point}, device_id_type=MESH)
+    for step in range(1, width):
+        pl.semaphore_signal(barrier, inc=1, device_id={"ga": lax.rem(me + step, width)}, device_id_type=MESH)
+    pl.semaphore_wait(barrier, width)
+    ring = pltpu.make_async_remote_copy(
+        src_ref=coef_hbm,
+        dst_ref=there_ref,
+        send_sem=ring_send,
+        recv_sem=ring_recv,
+        device_id={"ka": lax.rem(point + 1, count)},
+        device_id_type=MESH,
+    )
+    ring.start()
+    fetch[0].wait()
+    fetch[1].wait()
     waves = vec_ref.shape[1]
     index = vec_ref[...]
     cut_x = index // PLANE
     cut_n = index % PLANE
     points = lax.broadcasted_iota(jnp.int32, (PLANE, waves), 0)
     onehot = jnp.where(points == cut_n, 1.0 / 64, 0.0).astype(BF)
-    coefs = [
-        jnp.concatenate([here_ref[:, c, :], there_ref[:, c, :]], axis=0) for c in range(2)
-    ]
-    for j in range(4):
-        masks = [(cut_x == 4 * j + i).astype(F32).astype(BF) for i in range(4)]
-        block = jnp.concatenate([coefs[c] * masks[i] for c in range(2) for i in range(4)], axis=0)
-        field = lax.dot_general(onehot, block, (((1,), (1,)), ((), ())), preferred_element_type=F32)
-        pre[pl.ds(j * PLANE, PLANE), :] = field[:, :LANES]
-        pim[pl.ds(j * PLANE, PLANE), :] = field[:, LANES:]
+    for j in (0, 2):
+        own[:, pl.ds(j * LANES, 2 * LANES)] = scattered(here_ref, cut_x, onehot, j)
+    ring.wait()
+    lower = lax.broadcasted_iota(jnp.int32, (PLANE, LANES), 1) < PAIRS
+    for j in (0, 2):
+        other = scattered(there_ref, cut_x, onehot, j)
+        for e in range(2):
+            mine = own[:, pl.ds((j + e) * LANES, LANES)]
+            far = other[:, e * LANES:(e + 1) * LANES]
+            pre[pl.ds((j + e) * PLANE, PLANE), :] = jnp.where(lower, mine, pltpu.roll(far, PAIRS, 1))
+            pim[pl.ds((j + e) * PLANE, PLANE), :] = jnp.where(lower, pltpu.roll(mine, PAIRS, 1), far)
 
     @pl.loop(0, 8)
     def _(step):
@@ -134,6 +173,8 @@
             pre[pl.ds(base + z * 8, 8), :] = re
             pim[pl.ds(base + z * 8, 8), :] = im
 
+    for copy in fetch[2:]:
+        copy.wait()
     quarters = [(pre[pl.ds(j * PLANE, PLANE), :], pim[pl.ds(j * PLANE, PLANE), :]) for j in range(4)]
     for k1, (re, im) in enumerate(radix4(quarters, 1)):
         high, low = split(jnp.concatenate([re, im], axis=1))
@@ -187,7 +228,7 @@
             g = step * 32 + u
             vpick[pl.ds(g, 1), :] = vgrid[pl.ds(idx_ref[g], 1), :]
 
-    start = lax.axis_index("ga") * strip
+    start = me * strip
 
     @pl.loop(0, strip // 32)
     def _(step):
@@ -200,22 +241,14 @@
     cross = jnp.dot(left, screened, preferred_element_type=F32)
     top, bottom = cross[:PAIRS], pltpu.roll(cross[PAIRS:], PAIRS, 1)
     lane = lax.broadcasted_iota(jnp.int32, (PAIRS, LANES), 1)
-    total = jnp.where(lane < PAIRS, top + bottom, top - bottom) * (1.0 / math.sqrt(waves))
-    for d in range(PAIRS // rows):
-        out_ref[d] = total[d * rows:(d + 1) * rows]
-
-
-def scatter_sum(width, x_ref, out_ref, slots, send_sem, recv_sem):
-    me = lax.axis_index("ga")
-    barrier = pltpu.get_barrier_semaphore()
-    for step in range(1, width):
-        pl.semaphore_signal(barrier, inc=1, device_id={"ga": lax.rem(me + step, width)}, device_id_type=MESH)
-    pl.semaphore_wait(barrier, width - 1)
+    total = jnp.where(lane < PAIRS, top + bottom, top - bottom)
+    for d in range(width):
+        blocks[d] = total[d * rows:(d + 1) * rows]
     copies = []
     for step in range(1, width):
         peer = lax.rem(me + step, width)
         copy = pltpu.make_async_remote_copy(
-            src_ref=x_ref.at[peer],
+            src_ref=blocks.at[peer],
             dst_ref=slots.at[step - 1],
             send_sem=send_sem.at[step - 1],
             recv_sem=recv_sem.at[step - 1],
@@ -224,7 +257,7 @@
         )
         copy.start()
         copies.append(copy)
-    total = x_ref[me]
+    total = blocks[me]
     for step, copy in enumerate(copies):
         copy.wait_recv()
         total = total + slots[step]
@@ -239,16 +272,23 @@
     strip, waves = screening.shape[1:]
     rows = PAIRS // width
     here = band_coefs[0]
-    there = lax.ppermute(here, "ka", [(i, (i + 1) % count) for i in range(count)])
-    high, low, spread = tables()
-    vmem = pl.BlockSpec(memory_space=pltpu.VMEM)
-    smem = pl.BlockSpec(memory_space=pltpu.SMEM)
-    terms = pl.pallas_call(
-        functools.partial(compute, strip, rows),
-        out_shape=jax.ShapeDtypeStruct((width, rows, LANES), F32),
-        in_specs=[vmem, vmem, vmem, smem, vmem, vmem, vmem, vmem],
-        out_specs=vmem,
+    high, low, spread = (jnp.asarray(t) for t in tables())
+    hbm = pl.BlockSpec(memory_space=pltpu.HBM)
+    result = pl.pallas_call(
+        functools.partial(compute, width, count, strip, rows),
+        out_shape=jax.ShapeDtypeStruct((rows, LANES), F32),
+        in_specs=[hbm] * 7,
+        out_specs=pl.BlockSpec(memory_space=pltpu.VMEM),
         scratch_shapes=[
+            pltpu.VMEM(here.shape, BF),
+            pltpu.VMEM(here.shape, BF),
+            pltpu.VMEM((1, waves), jnp.int32),
+            pltpu.SMEM((waves,), jnp.int32),
+            pltpu.VMEM((strip, waves), BF),
+            pltpu.VMEM(high.shape, BF),
+            pltpu.VMEM(low.shape, BF),
+            pltpu.VMEM(spread.shape, BF),
+            pltpu.VMEM((PLANE, 4 * LANES), F32),
             pltpu.VMEM((4 * PLANE, LANES), F32),
             pltpu.VMEM((4 * PLANE, LANES), F32),
             pltpu.VMEM((GRID, LANES), F32),
@@ -257,22 +297,19 @@
             pltpu.VMEM((GRID, LANES), F32),
             pltpu.VMEM((waves, LANES), F32),
             pltpu.VMEM((strip, LANES), F32),
-        ],
-        compiler_params=pltpu.CompilerParams(vmem_limit_bytes=48 * 1024 * 1024),
-    )(here, there, grid_index[None], grid_index, screening[0], jnp.asarray(high), jnp.asarray(low), jnp.asarray(spread))
-    result = pl.pallas_call(
-        functools.partial(scatter_sum, width),
-        out_shape=jax.ShapeDtypeStruct((rows, LANES), F32),
-        in_specs=[vmem],
-        out_specs=vmem,
-        scratch_shapes=[
+            pltpu.VMEM((width, rows, LANES), F32),
             pltpu.VMEM((width - 1, rows, LANES), F32),
+            pltpu.SemaphoreType.DMA((7,)),
+            pltpu.SemaphoreType.DMA,
+            pltpu.SemaphoreType.DMA,
             pltpu.SemaphoreType.DMA((width - 1,)),
             pltpu.SemaphoreType.DMA((width - 1,)),
         ],
-        compiler_params=pltpu.CompilerParams(collective_id=0, has_side_effects=True),
-    )(terms)
-    return result[None, None]
+        compiler_params=pltpu.CompilerParams(
+            collective_id=0, has_side_effects=True, vmem_limit_bytes=56 * 1024 * 1024
+        ),
+    )(here, grid_index[None], grid_index, screening[0], high, low, spread)
+    return (result * (1.0 / math.sqrt(waves)))[None, None]
 
 
 def solution(mesh):

time: 38.7 us -> 28.6 us (0.74)
  local copies, waits for them, and re-layouts: 8.2 us -> 0 us
  waiting for transfers between devices: 5.74 us -> 0 us
  Pallas kernels: 23.8 us -> 27 us
  other arithmetic: 0 us -> 1.3 us
  starting transfers between devices: 0.45 us -> 0 us
    unnamed x15 -> x0, local copies, waits for them, and re-layouts: 8.2 us -> none
    ppermute x1 -> x0, waiting for transfers between devices: 5.74 us -> none  [body(): lax.ppermute(here, 'ka', [(i, (i + 1) % count) for i in range(count)])]
    pallas_call x2 -> x1, Pallas kernels: 23.8 us -> 27 us  [body(): pl.pallas_call(functools.partial(compute, width, count, strip, rows), out...]
    broadcast_in_dim x0 -> x1, other arithmetic: none -> 1.3 us  [body(): return (result * (1.0 / math.sqrt(waves)))[None, None]]
    ppermute x1 -> x0, starting transfers between devices: 0.45 us -> none  [body(): lax.ppermute(here, 'ka', [(i, (i + 1) % count) for i in range(count)])]
  transfers between devices with their start and end apart: 1 -> 0, of which waited for: 1 -> 0; matrix products, arithmetic and copies ran while one was open for 0% -> 0% of each run, Pallas kernels for 0% -> 0%
where the time goes in v2:
time: 28.6 us; the launch traced here: 28.4 us
  Pallas kernels  27 us (94%)
  other arithmetic  1.3 us (5%)
    pallas_call x1, Pallas kernels, body(): pl.pallas_call(functools.partial(compute, width, count, strip, rows), out...  27 us
    broadcast_in_dim x1, other arithmetic, body(): return (result * (1.0 / math.sqrt(waves)))[None, None]  1.3 us

profile of v2, /device:TPU:0, one launch (start us, length us, event | category | flops | bytes accessed | tf_op | source)
XLA Modules:
  0.0 28.4 jit_solution(14926056551819483407)
XLA Ops:
  0.0 27.0 %shard_map.64 = f32[16,128]{1,0:T(8,128)} custom-call(bf16[16,2,2048]{2,1,0:T(2,128)(2,1)} %bitcast.6, s32[1,2048]{1,0:T(1,128)} %bitcast.7, s32[2048]{0:T(1024)} %idx_hbm.1, bf16[512,2048]{1,0:T(8,128)(2,1)} %bitcast.5, bf16[4,256,256]{2,1,0:T(8,128)(2,1)} %constant.8.clone.mh_hbm, bf16[4,256,256]{2,1,0:T(8,128)(2,1)} %constant.9.clone.ml_hbm, ...), custom_call_target="tpu_custom_call" | custom-call | tf_op jit(solution)/shard_map/pallas_call | solution.py:277
  27.1 1.3 %multiply_bitcast_fusion = f32[1,1,16,128]{3,2,1,0:T(8,128)} fusion(f32[16,128]{1,0:T(8,128)} %shard_map.64), kind=kLoop, calls=%fused_computation | loop fusion | flops 2048 | bytes 16384 | tf_op jit(solution)/shard_map/broadcast_in_dim | solution.py:312

commit v3 on v2

--- a/solution.py
+++ b/solution.py
@@ -155,19 +155,19 @@
             pre[pl.ds((j + e) * PLANE, PLANE), :] = jnp.where(lower, mine, pltpu.roll(far, PAIRS, 1))
             pim[pl.ds((j + e) * PLANE, PLANE), :] = jnp.where(lower, pltpu.roll(mine, PAIRS, 1), far)
 
-    @pl.loop(0, 8)
+    @pl.loop(0, 8, unroll=4)
     def _(step):
         base = (step // 2) * PLANE + (step % 2) * 8
         at = [pl.ds(pl.multiple_of(base + y * NFFT, 8), 8) for y in range(NFFT)]
         for y, (re, im) in enumerate(fft16([(pre[a, :], pim[a, :]) for a in at], 1)):
-            pre[at[y], :] = re
-            pim[at[y], :] = im
-
-    @pl.loop(0, 8)
+            qre[at[y], :] = re
+            qim[at[y], :] = im
+
+    @pl.loop(0, 8, unroll=4)
     def _(step):
         base = pl.multiple_of(step * 128, 128)
         got = fft16(
-            [(pre[pl.ds(base + z, 8, stride=NFFT), :], pim[pl.ds(base + z, 8, stride=NFFT), :]) for z in range(NFFT)], 1
+            [(qre[pl.ds(base + z, 8, stride=NFFT), :], qim[pl.ds(base + z, 8, stride=NFFT), :]) for z in range(NFFT)], 1
         )
         for z, (re, im) in enumerate(got):
             pre[pl.ds(base + z * 8, 8), :] = re
@@ -183,34 +183,33 @@
             + jnp.dot(low, mh_ref[k1], preferred_element_type=F32)
             + jnp.dot(high, ml_ref[k1], preferred_element_type=F32)
         )
-        left_re = jnp.concatenate(split(mixed[:, :LANES]), axis=1)
-        left_im = jnp.concatenate(split(mixed[:, LANES:]), axis=1)
+        both = jnp.concatenate([mixed[:, :LANES], mixed[:, LANES:]], axis=0)
+        lines = jnp.concatenate(split(both), axis=1)
         for g in range(4):
-            real = jnp.dot(left_re, e_ref[g], preferred_element_type=F32)
-            imag = jnp.dot(left_im, e_ref[g], preferred_element_type=F32)
-            ar, br = real[:, :LANES], real[:, LANES:]
-            ai, bi = imag[:, :LANES], imag[:, LANES:]
+            field = jnp.dot(lines, e_ref[g], preferred_element_type=F32)
+            ar, br = field[:PLANE, :LANES], field[:PLANE, LANES:]
+            ai, bi = field[PLANE:, :LANES], field[PLANE:, LANES:]
             at = pl.ds((k1 + 4 * g) * PLANE, PLANE)
             qre[at, :] = ar * br + ai * bi
             qim[at, :] = ar * bi - ai * br
 
-    @pl.loop(0, 32)
+    @pl.loop(0, 32, unroll=4)
     def _(step):
         at = [pl.ds(pl.multiple_of(x * PLANE + step * 8, 8), 8) for x in range(NFFT)]
         for x, (re, im) in enumerate(fft16([(qre[a, :], qim[a, :]) for a in at], -1)):
-            qre[at[x], :] = re
-            qim[at[x], :] = im
-
-    @pl.loop(0, 32)
+            vgrid[at[x], :] = re
+            cgrid[at[x], :] = im
+
+    @pl.loop(0, 32, unroll=4)
     def _(step):
         at = [pl.ds(pl.multiple_of(step * 128 + z * 8, 8), 8) for z in range(NFFT)]
-        for z, (re, im) in enumerate(fft16([(qre[a, :], qim[a, :]) for a in at], -1)):
+        for z, (re, im) in enumerate(fft16([(vgrid[a, :], cgrid[a, :]) for a in at], -1)):
             qre[at[z], :] = re
             qim[at[z], :] = im
 
     left_half = lax.broadcasted_iota(jnp.int32, (8, LANES), 1) < PAIRS
 
-    @pl.loop(0, 32)
+    @pl.loop(0, 32, unroll=4)
     def _(step):
         plane = (step // 2) * PLANE
         half = step % 2
@@ -224,16 +223,18 @@
 
     @pl.loop(0, waves // 32)
     def _(step):
+        base = pl.multiple_of(step * 32, 32)
         for u in range(32):
-            g = step * 32 + u
+            g = base + u
             vpick[pl.ds(g, 1), :] = vgrid[pl.ds(idx_ref[g], 1), :]
 
     start = me * strip
 
     @pl.loop(0, strip // 32)
     def _(step):
+        base = pl.multiple_of(step * 32, 32)
         for u in range(32):
-            g = step * 32 + u
+            g = base + u
             cpick[pl.ds(g, 1), :] = cgrid[pl.ds(idx_ref[start + g], 1), :]
 
     screened = jnp.dot(w_ref[...], vpick[...].astype(BF), preferred_element_type=F32).astype(BF)

time: 28.6 us -> 26.6 us (0.930)
  Pallas kernels: 27 us -> 25.1 us
    pallas_call x1, Pallas kernels: 27 us -> 25.1 us  [body(): pl.pallas_call(functools.partial(compute, width, count, strip, rows), out...]
where the time goes in v3:
time: 26.6 us; the launch traced here: 26.4 us
  Pallas kernels  25.1 us (94%)
  other arithmetic  1.3 us (5%)
    pallas_call x1, Pallas kernels, body(): pl.pallas_call(functools.partial(compute, width, count, strip, rows), out...  25.1 us
    broadcast_in_dim x1, other arithmetic, body(): return (result * (1.0 / math.sqrt(waves)))[None, None]  1.3 us

profile of v3, /device:TPU:0, one launch (start us, length us, event | category | flops | bytes accessed | tf_op | source)
XLA Modules:
  0.0 26.4 jit_solution(10659654488151885718)
XLA Ops:
  0.0 25.1 %shard_map.64 = f32[16,128]{1,0:T(8,128)} custom-call(bf16[16,2,2048]{2,1,0:T(2,128)(2,1)} %bitcast.6, s32[1,2048]{1,0:T(1,128)} %bitcast.7, s32[2048]{0:T(1024)} %idx_hbm.1, bf16[512,2048]{1,0:T(8,128)(2,1)} %bitcast.5, bf16[4,256,256]{2,1,0:T(8,128)(2,1)} %constant.8.clone.mh_hbm, bf16[4,256,256]{2,1,0:T(8,128)(2,1)} %constant.9.clone.ml_hbm, ...), custom_call_target="tpu_custom_call" | custom-call | tf_op jit(solution)/shard_map/pallas_call | solution.py:278
  25.1 1.3 %multiply_bitcast_fusion = f32[1,1,16,128]{3,2,1,0:T(8,128)} fusion(f32[16,128]{1,0:T(8,128)} %shard_map.64), kind=kLoop, calls=%fused_computation | loop fusion | flops 2048 | bytes 16384 | tf_op jit(solution)/shard_map/broadcast_in_dim | solution.py:313

commit v4 on v3

--- a/solution.py
+++ b/solution.py
@@ -69,12 +69,12 @@
 
 def tables():
     half = BANDS // 2
-    group = np.arange(LANES) // half % 4
-    band = np.arange(LANES) // PAIRS * half + np.arange(LANES) % half
+    group = np.arange(LANES) // half
+    band = np.arange(LANES) % half
     same = (band[:, None] == band[None, :]).astype(np.float64)
     mats = []
-    for k1 in range(4):
-        angle = 2.0 * np.pi * (group[:, None] * (k1 + 4 * group[None, :]) % 16) / 16
+    for k1 in range(2):
+        angle = 2.0 * np.pi * (group[:, None] * (k1 + 2 * group[None, :]) % 16) / 16
         c, s = np.cos(angle) * same, np.sin(angle) * same
         mats.append(np.block([[c, s], [-s, c]]))
     full = np.stack(mats).astype(np.float32)
@@ -82,15 +82,13 @@
     low = (full - high.astype(np.float32)).astype(BF)
     lane = np.arange(LANES)
     kind, pair = lane // PAIRS, lane % PAIRS
-    first = kind * NBND + pair // NBND
-    second = 2 * NBND + kind * NBND + pair % NBND
     spread = []
-    for g in range(4):
-        here = (group == g)[:, None]
-        block = np.concatenate(
-            [here & (band[:, None] == first[None, :]), here & (band[:, None] == second[None, :])], axis=1
-        )
-        spread.append(np.concatenate([block, block], axis=0) * 0.125)
+    for wanted in (kind * NBND + pair // NBND, kind * NBND + pair % NBND):
+        for g in range(0, 8, 2):
+            block = np.concatenate(
+                [(group == g + e)[:, None] & (band[:, None] == wanted[None, :]) for e in range(2)], axis=1
+            )
+            spread.append(np.concatenate([block, block], axis=0) * 0.125)
     return high, low, np.stack(spread).astype(BF)
 
 
@@ -99,19 +97,53 @@
     return high, (value - high.astype(F32)).astype(BF)
 
 
-def scattered(coef_ref, cut_x, onehot, first):
+def orbitals(coef_ref, cut_x, onehot, pre, pim, tre, tim, mh_ref, ml_ref, e_ref, side, use):
     parts = [coef_ref[:, c, :] for c in range(2)]
-    block = []
-    for j in (first, first + 1):
-        masks = [(cut_x == 4 * j + i).astype(F32).astype(BF) for i in range(4)]
-        block += [parts[c] * masks[i] for c in range(2) for i in range(4)]
-    block = jnp.concatenate(block, axis=0)
-    return lax.dot_general(onehot, block, (((1,), (1,)), ((), ())), preferred_element_type=F32)
+    for j in range(2):
+        masks = [(cut_x == 8 * j + i).astype(F32).astype(BF) for i in range(8)]
+        block = jnp.concatenate([parts[c] * masks[i] for c in range(2) for i in range(8)], axis=0)
+        field = lax.dot_general(onehot, block, (((1,), (1,)), ((), ())), preferred_element_type=F32)
+        pre[pl.ds(j * PLANE, PLANE), :] = field[:, :LANES]
+        pim[pl.ds(j * PLANE, PLANE), :] = field[:, LANES:]
+
+    @pl.loop(0, 4, unroll=4)
+    def _(step):
+        base = (step // 2) * PLANE + (step % 2) * 8
+        at = [pl.ds(pl.multiple_of(base + y * NFFT, 8), 8) for y in range(NFFT)]
+        for y, (re, im) in enumerate(fft16([(pre[a, :], pim[a, :]) for a in at], 1)):
+            tre[at[y], :] = re
+            tim[at[y], :] = im
+
+    @pl.loop(0, 4, unroll=4)
+    def _(step):
+        base = pl.multiple_of(step * 128, 128)
+        got = fft16(
+            [(tre[pl.ds(base + z, 8, stride=NFFT), :], tim[pl.ds(base + z, 8, stride=NFFT), :]) for z in range(NFFT)], 1
+        )
+        for z, (re, im) in enumerate(got):
+            pre[pl.ds(base + z * 8, 8), :] = re
+            pim[pl.ds(base + z * 8, 8), :] = im
+
+    halves = [jnp.concatenate([pre[pl.ds(j * PLANE, PLANE), :], pim[pl.ds(j * PLANE, PLANE), :]], axis=1) for j in range(2)]
+    for k1, field in enumerate((halves[0] + halves[1], halves[0] - halves[1])):
+        high, low = split(field)
+        mixed = (
+            jnp.dot(high, mh_ref[k1], preferred_element_type=F32)
+            + jnp.dot(low, mh_ref[k1], preferred_element_type=F32)
+            + jnp.dot(high, ml_ref[k1], preferred_element_type=F32)
+        )
+        both = jnp.concatenate([mixed[:, :LANES], mixed[:, LANES:]], axis=0)
+        lines = jnp.concatenate(split(both), axis=1)
+        for h in range(4):
+            got = jnp.dot(lines, e_ref[4 * side + h], preferred_element_type=F32)
+            for e in range(2):
+                column = got[:, e * LANES:(e + 1) * LANES]
+                use(k1 + 2 * (2 * h + e), column[:PLANE], column[PLANE:])
 
 
 def compute(width, count, strip, rows, coef_hbm, vec_hbm, idx_hbm, w_hbm, mh_hbm, ml_hbm, e_hbm, out_ref,
             here_ref, there_ref, vec_ref, idx_ref, w_ref, mh_ref, ml_ref, e_ref,
-            own, pre, pim, qre, qim, vgrid, cgrid, vpick, cpick, blocks, slots,
+            ore, oim, pre, pim, qre, qim, vgrid, cgrid, vpick, cpick, blocks, slots,
             in_sem, ring_send, ring_recv, send_sem, recv_sem):
     me = lax.axis_index("ga")
     point = lax.axis_index("ka")
@@ -143,55 +175,22 @@
     cut_n = index % PLANE
     points = lax.broadcasted_iota(jnp.int32, (PLANE, waves), 0)
     onehot = jnp.where(points == cut_n, 1.0 / 64, 0.0).astype(BF)
-    for j in (0, 2):
-        own[:, pl.ds(j * LANES, 2 * LANES)] = scattered(here_ref, cut_x, onehot, j)
-    ring.wait()
-    lower = lax.broadcasted_iota(jnp.int32, (PLANE, LANES), 1) < PAIRS
-    for j in (0, 2):
-        other = scattered(there_ref, cut_x, onehot, j)
-        for e in range(2):
-            mine = own[:, pl.ds((j + e) * LANES, LANES)]
-            far = other[:, e * LANES:(e + 1) * LANES]
-            pre[pl.ds((j + e) * PLANE, PLANE), :] = jnp.where(lower, mine, pltpu.roll(far, PAIRS, 1))
-            pim[pl.ds((j + e) * PLANE, PLANE), :] = jnp.where(lower, pltpu.roll(mine, PAIRS, 1), far)
-
-    @pl.loop(0, 8, unroll=4)
-    def _(step):
-        base = (step // 2) * PLANE + (step % 2) * 8
-        at = [pl.ds(pl.multiple_of(base + y * NFFT, 8), 8) for y in range(NFFT)]
-        for y, (re, im) in enumerate(fft16([(pre[a, :], pim[a, :]) for a in at], 1)):
-            qre[at[y], :] = re
-            qim[at[y], :] = im
-
-    @pl.loop(0, 8, unroll=4)
-    def _(step):
-        base = pl.multiple_of(step * 128, 128)
-        got = fft16(
-            [(qre[pl.ds(base + z, 8, stride=NFFT), :], qim[pl.ds(base + z, 8, stride=NFFT), :]) for z in range(NFFT)], 1
-        )
-        for z, (re, im) in enumerate(got):
-            pre[pl.ds(base + z * 8, 8), :] = re
-            pim[pl.ds(base + z * 8, 8), :] = im
-
     for copy in fetch[2:]:
         copy.wait()
-    quarters = [(pre[pl.ds(j * PLANE, PLANE), :], pim[pl.ds(j * PLANE, PLANE), :]) for j in range(4)]
-    for k1, (re, im) in enumerate(radix4(quarters, 1)):
-        high, low = split(jnp.concatenate([re, im], axis=1))
-        mixed = (
-            jnp.dot(high, mh_ref[k1], preferred_element_type=F32)
-            + jnp.dot(low, mh_ref[k1], preferred_element_type=F32)
-            + jnp.dot(high, ml_ref[k1], preferred_element_type=F32)
-        )
-        both = jnp.concatenate([mixed[:, :LANES], mixed[:, LANES:]], axis=0)
-        lines = jnp.concatenate(split(both), axis=1)
-        for g in range(4):
-            field = jnp.dot(lines, e_ref[g], preferred_element_type=F32)
-            ar, br = field[:PLANE, :LANES], field[:PLANE, LANES:]
-            ai, bi = field[PLANE:, :LANES], field[PLANE:, LANES:]
-            at = pl.ds((k1 + 4 * g) * PLANE, PLANE)
-            qre[at, :] = ar * br + ai * bi
-            qim[at, :] = ar * bi - ai * br
+
+    def keep(x, re, im):
+        ore[pl.ds(x * PLANE, PLANE), :] = re
+        oim[pl.ds(x * PLANE, PLANE), :] = im
+
+    def multiply(x, re, im):
+        at = pl.ds(x * PLANE, PLANE)
+        ar, ai = ore[at, :], oim[at, :]
+        qre[at, :] = ar * re + ai * im
+        qim[at, :] = ar * im - ai * re
+
+    orbitals(here_ref, cut_x, onehot, pre, pim, vgrid, cgrid, mh_ref, ml_ref, e_ref, 0, keep)
+    ring.wait()
+    orbitals(there_ref, cut_x, onehot, pre, pim, vgrid, cgrid, mh_ref, ml_ref, e_ref, 1, multiply)
 
     @pl.loop(0, 32, unroll=4)
     def _(step):
@@ -289,9 +288,10 @@
             pltpu.VMEM(high.shape, BF),
             pltpu.VMEM(low.shape, BF),
             pltpu.VMEM(spread.shape, BF),
-            pltpu.VMEM((PLANE, 4 * LANES), F32),
-            pltpu.VMEM((4 * PLANE, LANES), F32),
-            pltpu.VMEM((4 * PLANE, LANES), F32),
+            pltpu.VMEM((GRID, LANES), F32),
+            pltpu.VMEM((GRID, LANES), F32),
+            pltpu.VMEM((2 * PLANE, LANES), F32),
+            pltpu.VMEM((2 * PLANE, LANES), F32),
             pltpu.VMEM((GRID, LANES), F32),
             pltpu.VMEM((GRID, LANES), F32),
             pltpu.VMEM((GRID, LANES), F32),

time: 26.6 us -> 25 us (0.940)
  Pallas kernels: 25.1 us -> 23.5 us
    pallas_call x1, Pallas kernels: 25.1 us -> 23.5 us  [body(): pl.pallas_call(functools.partial(compute, width, count, strip, rows), out...]
where the time goes in v4:
time: 25 us; the launch traced here: 24.8 us
  Pallas kernels  23.5 us (94%)
  other arithmetic  1.3 us (5%)
    pallas_call x1, Pallas kernels, body(): pl.pallas_call(functools.partial(compute, width, count, strip, rows), out...  23.5 us
    broadcast_in_dim x1, other arithmetic, body(): return (result * (1.0 / math.sqrt(waves)))[None, None]  1.3 us

profile of v4, /device:TPU:0, one launch (start us, length us, event | category | flops | bytes accessed | tf_op | source)
XLA Modules:
  0.0 24.8 jit_solution(16547129205814285860)
XLA Ops:
  0.0 23.5 %shard_map.64 = f32[16,128]{1,0:T(8,128)} custom-call(bf16[16,2,2048]{2,1,0:T(2,128)(2,1)} %bitcast.6, s32[1,2048]{1,0:T(1,128)} %bitcast.7, s32[2048]{0:T(1024)} %idx_hbm.1, bf16[512,2048]{1,0:T(8,128)(2,1)} %bitcast.5, bf16[2,256,256]{2,1,0:T(8,128)(2,1)} %constant.8.clone.mh_hbm, bf16[2,256,256]{2,1,0:T(8,128)(2,1)} %constant.9.clone.ml_hbm, ...), custom_call_target="tpu_custom_call" | custom-call | tf_op jit(solution)/shard_map/pallas_call | solution.py:277
  23.5 1.3 %multiply_bitcast_fusion = f32[1,1,16,128]{3,2,1,0:T(8,128)} fusion(f32[16,128]{1,0:T(8,128)} %shard_map.64), kind=kLoop, calls=%fused_computation | loop fusion | flops 2048 | bytes 16384 | tf_op jit(solution)/shard_map/broadcast_in_dim | solution.py:313

commit v5 on v4

--- a/solution.py
+++ b/solution.py
@@ -97,14 +97,22 @@
     return high, (value - high.astype(F32)).astype(BF)
 
 
-def orbitals(coef_ref, cut_x, onehot, pre, pim, tre, tim, mh_ref, ml_ref, e_ref, side, use):
-    parts = [coef_ref[:, c, :] for c in range(2)]
+def orbitals(coef_ref, cut_x, onehot, pre, pim, tre, tim, mh_ref, ml_ref, e_ref, side, use, arrive):
+    waves = cut_x.shape[1]
+    chunk = waves // len(arrive)
+    fields = [None, None]
+    for n, ready in enumerate(arrive):
+        ready()
+        at = slice(n * chunk, (n + 1) * chunk)
+        parts = [coef_ref[:, c, at] for c in range(2)]
+        for j in range(2):
+            masks = [(cut_x[:, at] == 8 * j + i).astype(F32).astype(BF) for i in range(8)]
+            block = jnp.concatenate([parts[c] * masks[i] for c in range(2) for i in range(8)], axis=0)
+            got = lax.dot_general(onehot[:, at], block, (((1,), (1,)), ((), ())), preferred_element_type=F32)
+            fields[j] = got if n == 0 else fields[j] + got
     for j in range(2):
-        masks = [(cut_x == 8 * j + i).astype(F32).astype(BF) for i in range(8)]
-        block = jnp.concatenate([parts[c] * masks[i] for c in range(2) for i in range(8)], axis=0)
-        field = lax.dot_general(onehot, block, (((1,), (1,)), ((), ())), preferred_element_type=F32)
-        pre[pl.ds(j * PLANE, PLANE), :] = field[:, :LANES]
-        pim[pl.ds(j * PLANE, PLANE), :] = field[:, LANES:]
+        pre[pl.ds(j * PLANE, PLANE), :] = fields[j][:, :LANES]
+        pim[pl.ds(j * PLANE, PLANE), :] = fields[j][:, LANES:]
 
     @pl.loop(0, 4, unroll=4)
     def _(step):
@@ -150,23 +158,29 @@
     pairs = [(vec_hbm, vec_ref), (coef_hbm, here_ref), (idx_hbm, idx_ref), (mh_hbm, mh_ref), (ml_hbm, ml_ref),
              (e_hbm, e_ref), (w_hbm, w_ref)]
     fetch = [pltpu.make_async_copy(src, dst, in_sem.at[n]) for n, (src, dst) in enumerate(pairs)]
-    for copy in fetch:
-        copy.start()
     barrier = pltpu.get_barrier_semaphore()
     left_point = lax.rem(point + count - 1, count)
     pl.semaphore_signal(barrier, inc=1, device_id={"ka": left_point}, device_id_type=MESH)
     for step in range(1, width):
         pl.semaphore_signal(barrier, inc=1, device_id={"ga": lax.rem(me + step, width)}, device_id_type=MESH)
+    for copy in fetch[:2]:
+        copy.start()
     pl.semaphore_wait(barrier, width)
-    ring = pltpu.make_async_remote_copy(
-        src_ref=coef_hbm,
-        dst_ref=there_ref,
-        send_sem=ring_send,
-        recv_sem=ring_recv,
-        device_id={"ka": lax.rem(point + 1, count)},
-        device_id_type=MESH,
-    )
-    ring.start()
+    bands, chunk = coef_hbm.shape[0] // 2, coef_hbm.shape[2] // 2
+    ring = []
+    for n in range(4):
+        at = (pl.ds(n % 2 * bands, bands), slice(None), pl.ds(n // 2 * chunk, chunk))
+        ring.append(pltpu.make_async_remote_copy(
+            src_ref=coef_hbm.at[at],
+            dst_ref=there_ref.at[at],
+            send_sem=ring_send.at[n],
+            recv_sem=ring_recv.at[n],
+            device_id={"ka": lax.rem(point + 1, count)},
+            device_id_type=MESH,
+        ))
+        ring[n].start()
+    for copy in fetch[2:]:
+        copy.start()
     fetch[0].wait()
     fetch[1].wait()
     waves = vec_ref.shape[1]
@@ -188,9 +202,9 @@
         qre[at, :] = ar * re + ai * im
         qim[at, :] = ar * im - ai * re
 
-    orbitals(here_ref, cut_x, onehot, pre, pim, vgrid, cgrid, mh_ref, ml_ref, e_ref, 0, keep)
-    ring.wait()
-    orbitals(there_ref, cut_x, onehot, pre, pim, vgrid, cgrid, mh_ref, ml_ref, e_ref, 1, multiply)
+    orbitals(here_ref, cut_x, onehot, pre, pim, vgrid, cgrid, mh_ref, ml_ref, e_ref, 0, keep, [lambda: None])
+    orbitals(there_ref, cut_x, onehot, pre, pim, vgrid, cgrid, mh_ref, ml_ref, e_ref, 1, multiply,
+             [lambda: (ring[0].wait_recv(), ring[1].wait_recv()), lambda: (ring[2].wait_recv(), ring[3].wait_recv())])
 
     @pl.loop(0, 32, unroll=4)
     def _(step):
@@ -223,18 +237,18 @@
     @pl.loop(0, waves // 32)
     def _(step):
         base = pl.multiple_of(step * 32, 32)
+        got = [vgrid[pl.ds(idx_ref[base + u], 1), :] for u in range(32)]
         for u in range(32):
-            g = base + u
-            vpick[pl.ds(g, 1), :] = vgrid[pl.ds(idx_ref[g], 1), :]
+            vpick[pl.ds(base + u, 1), :] = got[u]
 
     start = me * strip
 
     @pl.loop(0, strip // 32)
     def _(step):
         base = pl.multiple_of(step * 32, 32)
+        got = [cgrid[pl.ds(idx_ref[start + base + u], 1), :] for u in range(32)]
         for u in range(32):
-            g = base + u
-            cpick[pl.ds(g, 1), :] = cgrid[pl.ds(idx_ref[start + g], 1), :]
+            cpick[pl.ds(base + u, 1), :] = got[u]
 
     screened = jnp.dot(w_ref[...], vpick[...].astype(BF), preferred_element_type=F32).astype(BF)
     left = cpick[...].T.astype(BF)
@@ -262,7 +276,7 @@
         copy.wait_recv()
         total = total + slots[step]
     out_ref[...] = total
-    for copy in copies:
+    for copy in ring + copies:
         copy.wait_send()
 
 
@@ -301,8 +315,8 @@
             pltpu.VMEM((width, rows, LANES), F32),
             pltpu.VMEM((width - 1, rows, LANES), F32),
             pltpu.SemaphoreType.DMA((7,)),
-            pltpu.SemaphoreType.DMA,
-            pltpu.SemaphoreType.DMA,
+            pltpu.SemaphoreType.DMA((4,)),
+            pltpu.SemaphoreType.DMA((4,)),
             pltpu.SemaphoreType.DMA((width - 1,)),
             pltpu.SemaphoreType.DMA((width - 1,)),
         ],

time: 25 us -> 25.1 us (level)
  no operation moved by 1% of the time
where the time goes in v5:
time: 25.1 us; the launch traced here: 24.9 us
  Pallas kernels  23.6 us (94%)
  other arithmetic  1.3 us (5%)
    pallas_call x1, Pallas kernels, body(): pl.pallas_call(functools.partial(compute, width, count, strip, rows), out...  23.6 us
    broadcast_in_dim x1, other arithmetic, body(): return (result * (1.0 / math.sqrt(waves)))[None, None]  1.3 us

profile of v5, /device:TPU:0, one launch (start us, length us, event | category | flops | bytes accessed | tf_op | source)
XLA Modules:
  0.0 24.9 jit_solution(1663691571023163015)
XLA Ops:
  0.0 23.6 %shard_map.64 = f32[16,128]{1,0:T(8,128)} custom-call(bf16[16,2,2048]{2,1,0:T(2,128)(2,1)} %bitcast.6, s32[1,2048]{1,0:T(1,128)} %bitcast.7, s32[2048]{0:T(1024)} %idx_hbm.1, bf16[512,2048]{1,0:T(8,128)(2,1)} %bitcast.5, bf16[2,256,256]{2,1,0:T(8,128)(2,1)} %constant.8.clone.mh_hbm, bf16[2,256,256]{2,1,0:T(8,128)(2,1)} %constant.9.clone.ml_hbm, ...), custom_call_target="tpu_custom_call" | custom-call | tf_op jit(solution)/shard_map/pallas_call | solution.py:291
  23.6 1.3 %multiply_bitcast_fusion = f32[1,1,16,128]{3,2,1,0:T(8,128)} fusion(f32[16,128]{1,0:T(8,128)} %shard_map.64), kind=kLoop, calls=%fused_computation | loop fusion | flops 2048 | bytes 16384 | tf_op jit(solution)/shard_map/broadcast_in_dim | solution.py:327

commit v6 on v5

--- a/solution.py
+++ b/solution.py
@@ -97,7 +97,7 @@
     return high, (value - high.astype(F32)).astype(BF)
 
 
-def orbitals(coef_ref, cut_x, onehot, pre, pim, tre, tim, mh_ref, ml_ref, e_ref, side, use, arrive):
+def orbitals(coef_ref, cut_x, onehot, pre, pim, tre, tim, mh_ref, ml_ref, e_ref, side, use, arrive, settle):
     waves = cut_x.shape[1]
     chunk = waves // len(arrive)
     fields = [None, None]
@@ -132,6 +132,7 @@
             pre[pl.ds(base + z * 8, 8), :] = re
             pim[pl.ds(base + z * 8, 8), :] = im
 
+    settle()
     halves = [jnp.concatenate([pre[pl.ds(j * PLANE, PLANE), :], pim[pl.ds(j * PLANE, PLANE), :]], axis=1) for j in range(2)]
     for k1, field in enumerate((halves[0] + halves[1], halves[0] - halves[1])):
         high, low = split(field)
@@ -163,7 +164,7 @@
     pl.semaphore_signal(barrier, inc=1, device_id={"ka": left_point}, device_id_type=MESH)
     for step in range(1, width):
         pl.semaphore_signal(barrier, inc=1, device_id={"ga": lax.rem(me + step, width)}, device_id_type=MESH)
-    for copy in fetch[:2]:
+    for copy in fetch:
         copy.start()
     pl.semaphore_wait(barrier, width)
     bands, chunk = coef_hbm.shape[0] // 2, coef_hbm.shape[2] // 2
@@ -179,8 +180,6 @@
             device_id_type=MESH,
         ))
         ring[n].start()
-    for copy in fetch[2:]:
-        copy.start()
     fetch[0].wait()
     fetch[1].wait()
     waves = vec_ref.shape[1]
@@ -189,9 +188,6 @@
     cut_n = index % PLANE
     points = lax.broadcasted_iota(jnp.int32, (PLANE, waves), 0)
     onehot = jnp.where(points == cut_n, 1.0 / 64, 0.0).astype(BF)
-    for copy in fetch[2:]:
-        copy.wait()
-
     def keep(x, re, im):
         ore[pl.ds(x * PLANE, PLANE), :] = re
         oim[pl.ds(x * PLANE, PLANE), :] = im
@@ -202,9 +198,10 @@
         qre[at, :] = ar * re + ai * im
         qim[at, :] = ar * im - ai * re
 
-    orbitals(here_ref, cut_x, onehot, pre, pim, vgrid, cgrid, mh_ref, ml_ref, e_ref, 0, keep, [lambda: None])
+    orbitals(here_ref, cut_x, onehot, pre, pim, vgrid, cgrid, mh_ref, ml_ref, e_ref, 0, keep, [lambda: None],
+             lambda: [copy.wait() for copy in fetch[3:6]])
     orbitals(there_ref, cut_x, onehot, pre, pim, vgrid, cgrid, mh_ref, ml_ref, e_ref, 1, multiply,
-             [lambda: (ring[0].wait_recv(), ring[1].wait_recv()), lambda: (ring[2].wait_recv(), ring[3].wait_recv())])
+             [lambda: (ring[0].wait_recv(), ring[1].wait_recv()), lambda: (ring[2].wait_recv(), ring[3].wait_recv())], lambda: None)
 
     @pl.loop(0, 32, unroll=4)
     def _(step):
@@ -234,6 +231,8 @@
             vgrid[at, :] = jnp.where(left_half, re, pltpu.roll(im, PAIRS, 1))
             cgrid[at, :] = jnp.where(left_half, pltpu.roll(re, PAIRS, 1), im)
 
+    fetch[2].wait()
+
     @pl.loop(0, waves // 32)
     def _(step):
         base = pl.multiple_of(step * 32, 32)
@@ -250,6 +249,7 @@
         for u in range(32):
             cpick[pl.ds(base + u, 1), :] = got[u]
 
+    fetch[6].wait()
     screened = jnp.dot(w_ref[...], vpick[...].astype(BF), preferred_element_type=F32).astype(BF)
     left = cpick[...].T.astype(BF)
     cross = jnp.dot(left, screened, preferred_element_type=F32)

time: 25.1 us -> 24.9 us (level)
  no operation moved by 1% of the time
where the time goes in v6:
time: 24.9 us; the launch traced here: 24.7 us
  Pallas kernels  23.4 us (94%)
  other arithmetic  1.3 us (5%)
    pallas_call x1, Pallas kernels, body(): pl.pallas_call(functools.partial(compute, width, count, strip, rows), out...  23.4 us
    broadcast_in_dim x1, other arithmetic, body(): return (result * (1.0 / math.sqrt(waves)))[None, None]  1.3 us

profile of v6, /device:TPU:0, one launch (start us, length us, event | category | flops | bytes accessed | tf_op | source)
XLA Modules:
  0.0 24.7 jit_solution(10420665605815138753)
XLA Ops:
  0.0 23.4 %shard_map.64 = f32[16,128]{1,0:T(8,128)} custom-call(bf16[16,2,2048]{2,1,0:T(2,128)(2,1)} %bitcast.6, s32[1,2048]{1,0:T(1,128)} %bitcast.7, s32[2048]{0:T(1024)} %idx_hbm.1, bf16[512,2048]{1,0:T(8,128)(2,1)} %bitcast.5, bf16[2,256,256]{2,1,0:T(8,128)(2,1)} %constant.8.clone.mh_hbm, bf16[2,256,256]{2,1,0:T(8,128)(2,1)} %constant.9.clone.ml_hbm, ...), custom_call_target="tpu_custom_call" | custom-call | tf_op jit(solution)/shard_map/pallas_call | solution.py:291
  23.4 1.3 %multiply_bitcast_fusion = f32[1,1,16,128]{3,2,1,0:T(8,128)} fusion(f32[16,128]{1,0:T(8,128)} %shard_map.64), kind=kLoop, calls=%fused_computation | loop fusion | flops 2048 | bytes 16384 | tf_op jit(solution)/shard_map/broadcast_in_dim | solution.py:327

commit v7 on v6

--- a/solution.py
+++ b/solution.py
@@ -16,6 +16,7 @@
 PAIRS = NBND * NBND
 LANES = 2 * PAIRS
 BANDS = 4 * NBND
+SKEW = 9
 BF = jnp.bfloat16
 F32 = jnp.float32
 MESH = pl.DeviceIdType.MESH
@@ -214,17 +215,19 @@
     def _(step):
         at = [pl.ds(pl.multiple_of(step * 128 + z * 8, 8), 8) for z in range(NFFT)]
         for z, (re, im) in enumerate(fft16([(vgrid[a, :], cgrid[a, :]) for a in at], -1)):
-            qre[at[z], :] = re
-            qim[at[z], :] = im
+            to = pl.ds(step * 16 * SKEW + z * SKEW, 8)
+            qre[to, :] = re
+            qim[to, :] = im
 
     left_half = lax.broadcasted_iota(jnp.int32, (8, LANES), 1) < PAIRS
 
     @pl.loop(0, 32, unroll=4)
     def _(step):
         plane = (step // 2) * PLANE
+        skewed = (step // 2) * 32 * SKEW
         half = step % 2
         take = [
-            pl.ds(plane + (y // 8) * 128 + half * 64 + y % 8, 8, stride=8) for y in range(NFFT)
+            pl.ds(skewed + (y // 8) * 16 * SKEW + half * 8 * SKEW + y % 8, 8, stride=SKEW) for y in range(NFFT)
         ]
         for y, (re, im) in enumerate(fft16([(qre[a, :], qim[a, :]) for a in take], -1)):
             at = pl.ds(pl.multiple_of(plane + y * NFFT + half * 8, 8), 8)
@@ -306,8 +309,8 @@
             pltpu.VMEM((GRID, LANES), F32),
             pltpu.VMEM((2 * PLANE, LANES), F32),
             pltpu.VMEM((2 * PLANE, LANES), F32),
-            pltpu.VMEM((GRID, LANES), F32),
-            pltpu.VMEM((GRID, LANES), F32),
+            pltpu.VMEM((32 * 16 * SKEW, LANES), F32),
+            pltpu.VMEM((32 * 16 * SKEW, LANES), F32),
             pltpu.VMEM((GRID, LANES), F32),
             pltpu.VMEM((GRID, LANES), F32),
             pltpu.VMEM((waves, LANES), F32),

time: 24.9 us -> 24.7 us (level)
  no operation moved by 1% of the time
where the time goes in v7:
time: 24.7 us; the launch traced here: 24.5 us
  Pallas kernels  23.2 us (94%)
  other arithmetic  1.3 us (5%)
    pallas_call x1, Pallas kernels, body(): pl.pallas_call(functools.partial(compute, width, count, strip, rows), out...  23.2 us
    broadcast_in_dim x1, other arithmetic, body(): return (result * (1.0 / math.sqrt(waves)))[None, None]  1.3 us

profile of v7, /device:TPU:0, one launch (start us, length us, event | category | flops | bytes accessed | tf_op | source)
XLA Modules:
  0.0 24.5 jit_solution(16256440055173621314)
XLA Ops:
  0.0 23.2 %shard_map.64 = f32[16,128]{1,0:T(8,128)} custom-call(bf16[16,2,2048]{2,1,0:T(2,128)(2,1)} %bitcast.6, s32[1,2048]{1,0:T(1,128)} %bitcast.7, s32[2048]{0:T(1024)} %idx_hbm.1, bf16[512,2048]{1,0:T(8,128)(2,1)} %bitcast.5, bf16[2,256,256]{2,1,0:T(8,128)(2,1)} %constant.8.clone.mh_hbm, bf16[2,256,256]{2,1,0:T(8,128)(2,1)} %constant.9.clone.ml_hbm, ...), custom_call_target="tpu_custom_call" | custom-call | tf_op jit(solution)/shard_map/pallas_call | solution.py:294
  23.2 1.3 %multiply_bitcast_fusion = f32[1,1,16,128]{3,2,1,0:T(8,128)} fusion(f32[16,128]{1,0:T(8,128)} %shard_map.64), kind=kLoop, calls=%fused_computation | loop fusion | flops 2048 | bytes 16384 | tf_op jit(solution)/shard_map/broadcast_in_dim | solution.py:330

commit v8 on v7

--- a/solution.py
+++ b/solution.py
@@ -153,7 +153,7 @@
 
 def compute(width, count, strip, rows, coef_hbm, vec_hbm, idx_hbm, w_hbm, mh_hbm, ml_hbm, e_hbm, out_ref,
             here_ref, there_ref, vec_ref, idx_ref, w_ref, mh_ref, ml_ref, e_ref,
-            ore, oim, pre, pim, qre, qim, vgrid, cgrid, vpick, cpick, blocks, slots,
+            ore, oim, pre, pim, qre, qim, vgrid, cgrid, vpick, cpick, mixed, blocks, slots,
             in_sem, ring_send, ring_recv, send_sem, recv_sem):
     me = lax.axis_index("ga")
     point = lax.axis_index("ka")
@@ -236,13 +236,6 @@
 
     fetch[2].wait()
 
-    @pl.loop(0, waves // 32)
-    def _(step):
-        base = pl.multiple_of(step * 32, 32)
-        got = [vgrid[pl.ds(idx_ref[base + u], 1), :] for u in range(32)]
-        for u in range(32):
-            vpick[pl.ds(base + u, 1), :] = got[u]
-
     start = me * strip
 
     @pl.loop(0, strip // 32)
@@ -253,7 +246,28 @@
             cpick[pl.ds(base + u, 1), :] = got[u]
 
     fetch[6].wait()
-    screened = jnp.dot(w_ref[...], vpick[...].astype(BF), preferred_element_type=F32).astype(BF)
+    part = 2 * LANES
+
+    def pick(first):
+        for low in range(0, part, 32):
+            got = [vgrid[pl.ds(idx_ref[first + low + u], 1), :] for u in range(32)]
+            for u in range(32):
+                vpick[pl.ds(first + low + u, 1), :] = got[u]
+
+    def product(first):
+        piece = vpick[pl.ds(first, part), :].astype(BF)
+        return jnp.dot(w_ref[:, pl.ds(first, part)], piece, preferred_element_type=F32)
+
+    pick(0)
+    mixed[...] = jnp.zeros_like(mixed)
+
+    @pl.loop(0, waves // part - 1)
+    def _(step):
+        first = pl.multiple_of(step * part, part)
+        mixed[...] += product(first)
+        pick(pl.multiple_of(first + part, part))
+
+    screened = (mixed[...] + product(waves - part)).astype(BF)
     left = cpick[...].T.astype(BF)
     cross = jnp.dot(left, screened, preferred_element_type=F32)
     top, bottom = cross[:PAIRS], pltpu.roll(cross[PAIRS:], PAIRS, 1)
@@ -315,6 +329,7 @@
             pltpu.VMEM((GRID, LANES), F32),
             pltpu.VMEM((waves, LANES), F32),
             pltpu.VMEM((strip, LANES), F32),
+            pltpu.VMEM((strip, LANES), F32),
             pltpu.VMEM((width, rows, LANES), F32),
             pltpu.VMEM((width - 1, rows, LANES), F32),
             pltpu.SemaphoreType.DMA((7,)),

time: 24.7 us -> 24.8 us (level)
  no operation moved by 1% of the time
where the time goes in v8:
time: 24.8 us; the launch traced here: 24.6 us
  Pallas kernels  23.3 us (94%)
  other arithmetic  1.3 us (5%)
    pallas_call x1, Pallas kernels, body(): pl.pallas_call(functools.partial(compute, width, count, strip, rows), out...  23.3 us
    broadcast_in_dim x1, other arithmetic, body(): return (result * (1.0 / math.sqrt(waves)))[None, None]  1.3 us

profile of v8, /device:TPU:0, one launch (start us, length us, event | category | flops | bytes accessed | tf_op | source)
XLA Modules:
  0.0 24.6 jit_solution(17063174655757758206)
XLA Ops:
  0.0 23.3 %shard_map.64 = f32[16,128]{1,0:T(8,128)} custom-call(bf16[16,2,2048]{2,1,0:T(2,128)(2,1)} %bitcast.6, s32[1,2048]{1,0:T(1,128)} %bitcast.7, s32[2048]{0:T(1024)} %idx_hbm.1, bf16[512,2048]{1,0:T(8,128)(2,1)} %bitcast.5, bf16[2,256,256]{2,1,0:T(8,128)(2,1)} %constant.8.clone.mh_hbm, bf16[2,256,256]{2,1,0:T(8,128)(2,1)} %constant.9.clone.ml_hbm, ...), custom_call_target="tpu_custom_call" | custom-call | tf_op jit(solution)/shard_map/pallas_call | solution.py:308
  23.3 1.3 %multiply_bitcast_fusion = f32[1,1,16,128]{3,2,1,0:T(8,128)} fusion(f32[16,128]{1,0:T(8,128)} %shard_map.64), kind=kLoop, calls=%fused_computation | loop fusion | flops 2048 | bytes 16384 | tf_op jit(solution)/shard_map/broadcast_in_dim | solution.py:345
